TPU v7x, 256 devices: a whole 4x4x8 slice. The times are simulated.
256 devices in a mesh: resp: 8 (over y, z_hi), prompt: 32 (over x, z_lo, core).
Axes of the slice: x: 4, y: 4, z: 8 (z_hi: 2, z_lo: 4; z = z_hi * 4 + z_lo), core: 2. Of those that a mesh axis runs over, the one named last changes fastest.
Arguments:
- prompt_key_matrix: bfloat16 [512, 512], P('prompt'), may hold values from -4 to 4, as said below
- prompt_value_matrix: bfloat16 [512, 512], P('prompt'), may hold values from -15 to 15
- response_queries: bfloat16 [16, 2048, 2560], P('resp', 'prompt'), may hold values from -4 to 4, as said below
- response_cotangent: bfloat16 [16, 2048, 2560], P('resp', 'prompt'), may hold values from -0.08984375 to 0.08984375
- resp_keys: bfloat16 [16, 2048, 512], P('resp', 'prompt'), may hold values from -4 to 4, as said below
- resp_values: bfloat16 [16, 2048, 512], P('resp', 'prompt'), may hold values from -15 to 15
- thresholds: float32 [16, 2048, 20], P('resp', 'prompt'), may hold values from 0.8 to 1.6, as said below
- lengths: int32 [16], P('resp'), may hold values from 1 to 2048, as said below
Outputs:
- grad_queries: bfloat16 [16, 2048, 2560], P('resp', 'prompt')
- grad_resp_keys: bfloat16 [16, 2048, 512], P('resp', 'prompt')
- grad_resp_values: bfloat16 [16, 2048, 512], P('resp', 'prompt')
- grad_prompt_keys: bfloat16 [512, 512], P('prompt')
- grad_prompt_values: bfloat16 [512, 512], P('prompt')
Inputs may be any that keep to these rules, and one draw needn't show every extreme that they name: `prompt_key_matrix`: every entry is a multiple of 1/16. `response_queries`: every entry is a multiple of 1/16. `resp_keys`: every entry is a multiple of 1/16. `thresholds`: each threshold is an odd multiple of 1 / (512 sqrt(128)). `lengths`: in every draw some response has all 2048 positions.
All inputs are finite; a program needn't handle non-finite values.
Results may differ from a plain program's by a relative error of at most 0.024.
Values may be sent and summed in bfloat16 or wider, within the bound.
No kernel may reach another device: no remote copies, remote signals or barrier semaphores. Data moves between devices by JAX's collectives and lax.ppermute only.
A program may use at most 128 MiB of HBM per device.

v0:
```python
import functools

import jax
import jax.numpy as jnp
from jax import lax
from jax.experimental import pallas as pl
from jax.experimental.pallas import tpu as pltpu
from jax.sharding import Mesh
from jax.sharding import PartitionSpec as P

BF = jnp.bfloat16
F32 = jnp.float32
GROUP = 5
HD = 128
OWN = 64
SPAN = 2 * OWN
ROWS = GROUP * SPAN
WIDE = GROUP * HD
PACKED = 2 * WIDE + HD
PROMPT = 512
OWN_PROMPT = 16
KEYS = PROMPT + 2048
ROOT = HD**0.5
NT = (((1,), (1,)), ((), ()))
NN = (((1,), (0,)), ((), ()))
TN = (((0,), (0,)), ((), ()))


def call(body, out_shape, count, scratch=(), limit=None, name=None, scalars=0, flops=1000):
    vm = pl.BlockSpec(memory_space=pltpu.VMEM)
    return pl.pallas_call(
        body,
        out_shape=out_shape,
        in_specs=[pl.BlockSpec(memory_space=pltpu.SMEM)] * scalars + [vm] * count,
        out_specs=jax.tree.map(lambda _: vm, out_shape),
        scratch_shapes=scratch,
        cost_estimate=pl.CostEstimate(flops=flops, bytes_accessed=2 * 10**6, transcendentals=0),
        compiler_params=pltpu.CompilerParams(vmem_limit_bytes=limit),
        name=name,
    )


def pack_keys_kernel(k_ref, v_ref, pk_ref, pv_ref, out):
    for head in range(4):
        cols = slice(head * HD, (head + 1) * HD)
        for member in range(2):
            to = 2 * head + member
            out[to, 0:OWN, 0:HD] = k_ref[member, :, cols]
            out[to, 0:OWN, HD:] = v_ref[member, :, cols]
            out[to, OWN:, 0:HD] = pk_ref[:, cols]
            out[to, OWN:, HD:] = pv_ref[:, cols]


def pack_rows_kernel(q_ref, c_ref, t_ref, out):
    for head in range(4):
        cols = slice(head * WIDE, (head + 1) * WIDE)
        for member in range(2):
            to = 2 * head + member
            out[to, :, 0:WIDE] = q_ref[member, :, cols]
            out[to, :, WIDE : 2 * WIDE] = c_ref[member, :, cols]
            left = t_ref[member, head]
            for part in range(3):
                piece = left.astype(BF)
                out[to, :, 2 * WIDE + part * GROUP : 2 * WIDE + (part + 1) * GROUP] = piece
                left = left - piece.astype(F32)
            out[to, :, 2 * WIDE + 3 * GROUP :] = jnp.zeros((OWN, HD - 3 * GROUP), BF)


def attend_kernel(step, where, *refs):
    kvs, rows, grads, prompts, dq = refs[0:4], refs[4], refs[5:9], refs[9:11], refs[11]
    k_all, v_all, t_all, q_st, c_st, prob, grad, dk, dv, dq_t = refs[12:]
    half, core, length = where[0], where[1], where[2]

    def key_places(j):
        far, turned = j // 2, j % 2
        base = 256 * (half if far == 0 else 1 - half) + OWN * (core if turned == 0 else 1 - core)
        for e in range(8):
            at = pl.multiple_of(PROMPT + 512 * (e // 2) + SPAN * (e % 2) + base, OWN)
            yield e, pl.ds(at, OWN), pl.ds(OWN_PROMPT * (8 * j + e), OWN_PROMPT)

    for j in range(4):
        for e, at, slot in key_places(j):
            k_all[at] = kvs[j][e, 0:OWN, 0:HD]
            v_all[at] = kvs[j][e, 0:OWN, HD:]
            k_all[slot] = kvs[j][e, OWN:, 0:HD]
            v_all[slot] = kvs[j][e, OWN:, HD:]
    dk[...] = jnp.zeros_like(dk)
    dv[...] = jnp.zeros_like(dv)
    lane = lax.broadcasted_iota(jnp.int32, (1, SPAN), 1)
    origin = 256 * half + OWN * core
    place = jnp.where(lane < OWN, lane, lane + OWN)
    sub = lax.broadcasted_iota(jnp.int32, (512, SPAN), 0)
    barred = jnp.where(sub <= place + origin, 0.0, 1e30)

    def block(b, carry):
        start = b * 512 + origin

        @pl.when(start >= length)
        def _():
            dq[pl.ds(2 * b, 2)] = jnp.zeros((2, OWN, WIDE), BF)

        @pl.when(start < length)
        def _():
            for side in range(2):
                for h in range(GROUP):
                    to = slice(h * SPAN + side * OWN, h * SPAN + (side + 1) * OWN)
                    q_st[to] = rows[2 * b + side, :, h * HD : (h + 1) * HD]
                    c_st[to] = rows[2 * b + side, :, WIDE + h * HD : WIDE + (h + 1) * HD]
            pieces = jnp.concatenate(
                [rows[2 * b + side, :, 2 * WIDE :].astype(F32) for side in range(2)], 0
            ).T
            t_all[...] = (
                pieces[0:GROUP] + pieces[GROUP : 2 * GROUP] + pieces[2 * GROUP : 3 * GROUP]
            ) * ROOT
            live_row = start + place < length
            thr = jnp.concatenate(
                [jnp.where(live_row, t_all[h : h + 1], 1e30) for h in range(GROUP)], 1
            )

            def first(k0, count, bar, totals):
                over = (
                    lax.dot_general(
                        k_all[pl.ds(k0, count)], q_st[...], NT, preferred_element_type=F32
                    )
                    - bar
                )
                weight = jnp.maximum(over, 0.0).astype(BF)
                prob[pl.ds(k0, count)] = weight
                pg = lax.dot_general(
                    v_all[pl.ds(k0, count)], c_st[...], NT, preferred_element_type=F32
                )
                grad[pl.ds(k0, count)] = pg
                live = over > 0.0
                num, tot = totals
                num = num + jnp.sum(jnp.where(live, 1.0, 0.0).reshape(count // 8, 8, ROWS), 0)
                tot = tot + jnp.sum(jnp.where(live, pg, 0.0).reshape(count // 8, 8, ROWS), 0)
                dv[pl.ds(k0, count)] += lax.dot_general(
                    weight, c_st[...], NN, preferred_element_type=F32
                )
                return num, tot

            def main(i, totals):
                return first(pl.multiple_of(i * 2 * step, 2 * step), 2 * step, thr, totals)

            base = PROMPT + b * 512

            def tail(i, totals):
                bar = thr + jnp.concatenate([barred] * GROUP, 1)
                return first(pl.multiple_of(base, 512), 512, bar, totals)

            zero = jnp.zeros((8, ROWS), F32)
            pairs = (1 + b) // 2
            odd = (1 + b) - 2 * pairs
            last = pl.multiple_of(pairs * 2 * step, 2 * step)
            totals = lax.fori_loop(0, pairs, main, (zero, zero))
            totals = lax.fori_loop(0, odd, lambda i, t: first(last, step, thr, t), totals)
            num, tot = tail(0, totals)
            mean = jnp.sum(tot, 0, keepdims=True) / jnp.maximum(
                jnp.sum(num, 0, keepdims=True), 1.0
            )
            dq_t[...] = jnp.zeros_like(dq_t)

            def second(k0, count):
                centred = (grad[pl.ds(k0, count)] - mean).astype(BF)
                ds = jnp.where(prob[pl.ds(k0, count)] > 0, centred, jnp.zeros((), BF))
                dk[pl.ds(k0, count)] += lax.dot_general(
                    ds, q_st[...], NN, preferred_element_type=F32
                )
                dq_t[...] += lax.dot_general(
                    k_all[pl.ds(k0, count)], ds, TN, preferred_element_type=F32
                )

            def main2(i, carry):
                second(pl.multiple_of(i * 2 * step, 2 * step), 2 * step)
                return carry

            def odd2(i, carry):
                second(last, step)
                return carry

            lax.fori_loop(0, pairs, main2, 0)
            lax.fori_loop(0, odd, odd2, 0)
            second(pl.multiple_of(base, 512), 512)
            for h in range(GROUP):
                part = (dq_t[:, h * SPAN : (h + 1) * SPAN].T * (1.0 / ROOT)).astype(BF)
                for side in range(2):
                    dq[2 * b + side, :, h * HD : (h + 1) * HD] = part[side * OWN : (side + 1) * OWN]

        return carry

    lax.fori_loop(0, 4, block, 0)
    for j in range(4):
        for part, total in ((0, dk), (1, dv)):
            cols = slice(part * HD, (part + 1) * HD)
            for e, at, slot in key_places(j):
                grads[j][e, :, cols] = (total[at] * (1.0 / ROOT)).astype(BF)
            held = (total[128 * j : 128 * (j + 1)] * (1.0 / ROOT)).astype(BF)
            prompts[j % 2][j // 2 * 128 : (j // 2 + 1) * 128, cols] = held


def attend(where, kvs, rows):
    shape = jax.ShapeDtypeStruct
    return call(
        functools.partial(attend_kernel, 512),
        [shape((8, OWN, 2 * HD), BF)] * 4
        + [shape((256, 2 * HD), BF)] * 2
        + [shape((8, OWN, WIDE), BF)],
        5,
        [
            pltpu.VMEM((KEYS, HD), BF),
            pltpu.VMEM((KEYS, HD), BF),
            pltpu.VMEM((GROUP, SPAN), F32),
            pltpu.VMEM((ROWS, HD), BF),
            pltpu.VMEM((ROWS, HD), BF),
            pltpu.VMEM((KEYS, ROWS), BF),
            pltpu.VMEM((KEYS, ROWS), F32),
            pltpu.VMEM((KEYS, HD), F32),
            pltpu.VMEM((KEYS, HD), F32),
            pltpu.VMEM((HD, ROWS), F32),
        ],
        48 * 1024 * 1024,
        "attend",
        1,
        6 * 10**9,
    )(where, *kvs, rows)


def unpack_rows_kernel(got, out_q, out_k, out_v):
    for head in range(4):
        cols = slice(head * HD, (head + 1) * HD)
        for member in range(2):
            part = got.at[2 * head + member]
            out_q[member, :, head * WIDE : (head + 1) * WIDE] = part[:, 0:WIDE]
            out_k[member, :, cols] = part[:, WIDE : WIDE + HD]
            out_v[member, :, cols] = part[:, WIDE + HD :]


def unpack_prompt_kernel(got, out_k, out_v):
    for head in range(4):
        cols = slice(head * HD, (head + 1) * HD)
        total = got[2 * head].astype(F32) + got[2 * head + 1].astype(F32)
        out_k[:, cols] = total[:, 0:HD].astype(BF)
        out_v[:, cols] = total[:, HD:].astype(BF)


def swap(values):
    return lax.ppermute(values, "core", [(0, 1), (1, 0)])


def far(values):
    return lax.ppermute(values, "half", [(0, 1), (1, 0)])


def exchange(values):
    return lax.all_to_all(values, ("x", "near"), 0, 0, tiled=True)


def added(*parts):
    return functools.reduce(jnp.add, [p.astype(F32) for p in parts]).astype(BF)


def local(
    prompt_key_matrix,
    prompt_value_matrix,
    response_queries,
    response_cotangent,
    resp_keys,
    resp_values,
    thresholds,
    lengths,
):
    half, near, core = (lax.axis_index(name) for name in ("half", "near", "core"))
    length = lax.dynamic_index_in_dim(lengths, near, 0, keepdims=False)
    where = jnp.stack([half, core, length]).astype(jnp.int32)
    shape = jax.ShapeDtypeStruct
    packed = call(pack_keys_kernel, shape((8, 80, 2 * HD), BF), 4, name="pack_keys")(
        resp_keys, resp_values, prompt_key_matrix, prompt_value_matrix
    )
    keys_own = exchange(packed)
    thresh = jnp.transpose(thresholds.reshape(2, OWN, 4, GROUP), (0, 2, 1, 3))
    rows = call(pack_rows_kernel, shape((8, OWN, PACKED), BF), 3, name="pack_rows")(
        response_queries, response_cotangent, thresh
    )
    keys_far = far(keys_own)
    rows = exchange(rows)
    kvs = [keys_own, swap(keys_own), keys_far, swap(keys_far)]
    outs = attend(where, kvs, rows)
    grads, prompts, dq = outs[0:4], outs[4:6], outs[6]

    far_sum = added(grads[2], swap(grads[3]))
    prompt_sum = added(prompts[0], swap(prompts[1]))
    far_sum, prompt_sum = lax.optimization_barrier((far_sum, prompt_sum))
    key_sum = added(grads[0], swap(grads[1]), far(far_sum))
    corners = [
        lax.ppermute(part, ("hi", "half"), [(i, i ^ mask) for i in range(4)])
        for part, mask in ((prompt_sum[:128], 2), (prompt_sum[128:], 1), (prompt_sum[128:], 3))
    ]
    corners, key_sum = lax.optimization_barrier((corners, key_sum))
    prompt_sum = added(prompt_sum[:128], *corners)
    back = exchange(jnp.concatenate([dq, key_sum], 2))
    around = [
        lax.ppermute(prompt_sum, "y", [(i, (i + by) % 4) for i in range(4)]) for by in (1, 2, 3)
    ]
    prompt_sum = added(prompt_sum, *around).reshape(8, OWN_PROMPT, 2 * HD)
    back, prompt_sum = lax.optimization_barrier((back, prompt_sum))
    prompt_back = exchange(prompt_sum)
    grad_queries, grad_resp_keys, grad_resp_values = call(
        unpack_rows_kernel,
        [shape((2, OWN, 4 * WIDE), BF)] + [shape((2, OWN, 4 * HD), BF)] * 2,
        1,
        name="unpack_rows",
    )(back)
    grad_prompt_keys, grad_prompt_values = call(
        unpack_prompt_kernel, [shape((OWN_PROMPT, 4 * HD), BF)] * 2, 1, name="unpack_prompt"
    )(prompt_back)
    return (grad_queries, grad_resp_keys, grad_resp_values, grad_prompt_keys, grad_prompt_values)


def solution(mesh):
    axes = ("y", "hi", "x", "half", "near", "core")
    fine = Mesh(mesh.devices.reshape(4, 2, 4, 2, 2, 2), axes)
    group, line = axes[:2], axes[2:]
    by_row = P(group, line, None)
    return jax.shard_map(
        local,
        mesh=fine,
        in_specs=(P(line, None), P(line, None), by_row, by_row, by_row, by_row, by_row, P(group)),
        out_specs=(by_row, by_row, by_row, P(line, None), P(line, None)),
        check_vma=False,
    )
```

profile of v0, /device:TPU:24, one launch (start us, length us, event | category | flops | bytes accessed | tf_op | source)
XLA Modules:
  0.0 115.2 jit_solution(17283136013155797080)
XLA Ops:
  0.6 1.8 %pack_keys.1 = bf16[8,80,256]{2,1,0:T(8,128)(2,1)} custom-call(bf16[2,64,512]{2,1,0:T(8,128)(2,1)} %k_ref.1, bf16[2,64,512]{2,1,0:T(8,128)(2,1)} %v_ref.1, bf16[16,512]{1,0:T(8,128)(2,1)} %pk_ref.1, bf16[16,512]{1,0:T(8,128)(2,1)} %pv_ref.1), custom_call_target="tpu_custom_call" | custom-call | flops 1000 | bytes 2000000 | tf_op jit(solution)/shard_map/pack_keys/pallas_call | solution.py:276
  2.4 5.7 %all-to-all-start = ((bf16[8,80,256]{2,1,0:T(8,128)(2,1)}), bf16[8,80,256]{2,1,0:T(8,128)(2,1)S(1)}, u32[]{:S(2)}, u32[]{:S(2)}) async-start(bf16[8,80,256]{2,1,0:T(8,128)(2,1)} %pack_keys.1), calls=%async_computation | async-start | bytes 655360 | tf_op jit(solution)/shard_map/all_to_all | solution.py:255
  8.0 1.6 %copy.13 = f32[2,64,4,5]{3,1,2,0:T(8,128)} copy(f32[2,64,4,5]{1,0,3,2:T(2,128)} %bitcast.6) | data formatting | bytes 20480 | tf_op jit(solution)/shard_map/reshape | solution.py:280
  9.6 2.7 %pack_rows.1 = bf16[8,64,1408]{2,1,0:T(8,128)(2,1)} custom-call(bf16[2,64,2560]{2,1,0:T(8,128)(2,1)} %q_ref.1, bf16[2,64,2560]{2,1,0:T(8,128)(2,1)} %c_ref.1, f32[2,4,64,5]{3,2,1,0:T(8,128)} %bitcast.5), custom_call_target="tpu_custom_call" | custom-call | flops 1000 | bytes 2000000 | tf_op jit(solution)/shard_map/pack_rows/pallas_call | solution.py:281
  12.4 0.0 copy-start.2
  12.4 3.7 %all-to-all-done.refs_0_ = bf16[8,80,256]{2,1,0:T(8,128)(2,1)S(1)} async-done(((bf16[8,80,256]{2,1,0:T(8,128)(2,1)}), bf16[8,80,256]{2,1,0:T(8,128)(2,1)S(1)}, u32[]{:S(2)}, u32[]{:S(2)}) %all-to-all-start) | async-done | bytes 327712 | tf_op jit(solution)/shard_map/all_to_all | solution.py:255
  16.0 3.6 %all-to-all-start.1 = ((bf16[8,64,1408]{2,1,0:T(8,128)(2,1)}), bf16[8,64,1408]{2,1,0:T(8,128)(2,1)S(1)}, u32[]{:S(2)}, u32[]{:S(2)}) async-start(bf16[8,64,1408]{2,1,0:T(8,128)(2,1)} %pack_rows.1), calls=%async_computation.1 | async-start | bytes 2883584 | tf_op jit(solution)/shard_map/all_to_all | solution.py:255
  19.6 3.4 %collective-permute-start.1 = (bf16[8,80,256]{2,1,0:T(8,128)(2,1)S(1)}, bf16[8,80,256]{2,1,0:T(8,128)(2,1)S(1)}, u32[]{:S(2)}, u32[]{:S(2)}) collective-permute-start(bf16[8,80,256]{2,1,0:T(8,128)(2,1)S(1)} %all-to-all-done.refs_0_), channel_id=1, source_target_pairs={{0,4},{4,0},{1,5},{5,1},{2,6},{6,2},{3,7},{7,3},{8,12},{12,8},{9,1... | collective-permute-start | bytes 983048 | tf_op jit(solution)/shard_map/ppermute | solution.py:251
  23.0 0.0 collective-permute-start
  23.0 18.3 %collective-permute-done.1.refs_2_ = bf16[8,80,256]{2,1,0:T(8,128)(2,1)S(1)} collective-permute-done((bf16[8,80,256]{2,1,0:T(8,128)(2,1)S(1)}, bf16[8,80,256]{2,1,0:T(8,128)(2,1)S(1)}, u32[]{:S(2)}, u32[]{:S(2)}) %collective-permute-start.1) | collective-permute-done | bytes 327712 | tf_op jit(solution)/shard_map/ppermute | solution.py:251
  41.3 0.0 collective-permute-start.2
  41.3 0.0 copy-done.2
  41.3 0.6 dynamic_slice.4
  41.9 0.7 pad_add_fusion.where
  42.6 0.0 collective-permute-done.refs_1_
  42.6 0.3 collective-permute-done.2.refs_3_
  42.9 2.6 %all-to-all-done.1.refs_4_ = bf16[8,64,1408]{2,1,0:T(8,128)(2,1)S(1)} async-done(((bf16[8,64,1408]{2,1,0:T(8,128)(2,1)}), bf16[8,64,1408]{2,1,0:T(8,128)(2,1)S(1)}, u32[]{:S(2)}, u32[]{:S(2)}) %all-to-all-start.1) | async-done | bytes 1441824 | tf_op jit(solution)/shard_map/all_to_all | solution.py:255
  45.6 3.9 %attend.1 = (bf16[8,64,256]{2,1,0:T(8,128)(2,1)S(1)}, bf16[8,64,256]{2,1,0:T(8,128)(2,1)S(1)}, bf16[8,64,256]{2,1,0:T(8,128)(2,1)S(1)}, bf16[8,64,256]{2,1,0:T(8...) custom-call(s32[3]{0:T(128)S(1)} %pad_add_fusion.where, ...), custom_call_target="tpu_custom_call" | custom-call | flops 6000000000 | bytes 2000000 | tf_op jit(solution)/shard_map/attend/pallas_call | solution.py:203
  49.4 0.1 collective-permute-start.4
  49.5 0.5 collective-permute-start.3
  50.0 0.1 collective-permute-start.8
  50.1 0.7 collective-permute-done.4
  50.9 0.3 collective-permute-done.3
  51.3 0.1 add_convert_fusion.1
  51.3 0.1 collective-permute-start.9
  51.4 20.3 %collective-permute-start.7 = (bf16[128,256]{1,0:T(8,128)(2,1)S(1)}, bf16[128,256]{1,0:T(8,128)(2,1)S(1)}, u32[]{:S(2)}, u32[]{:S(2)}) collective-permute-start(bf16[128,256]{1,0:T(8,128)(2,1)S(1)} %get-tuple-element.45), channel_id=1, source_target_pairs={{0,36},{4,32},{32,4},{36,0},{1,37},{5,33},{33,5},{37,1},{2,38},{6,... | collective-permute-start | bytes 196616 | tf_op jit(solution)/shard_map/ppermute | solution.py:295
  71.7 0.8 collective-permute-start.6
  72.5 1.7 %collective-permute-start.5 = (bf16[128,256]{1,0:T(8,128)(2,1)S(1)}, bf16[128,256]{1,0:T(8,128)(2,1)S(1)}, u32[]{:S(2)}, u32[]{:S(2)}) collective-permute-start(bf16[128,256]{1,0:T(8,128)(2,1)S(1)} %get-tuple-element.46), channel_id=1, source_target_pairs={{0,32},{4,36},{32,0},{36,4},{1,33},{5,37},{33,1},{37,5},{2,34},{6,... | collective-permute-start | bytes 196616 | tf_op jit(solution)/shard_map/ppermute | solution.py:295
  74.2 0.0 collective-permute-done.8
  74.2 0.0 collective-permute-done.9
  74.2 0.1 add_convert_fusion
  74.3 9.7 %collective-permute-done.5 = bf16[128,256]{1,0:T(8,128)(2,1)S(1)} collective-permute-done((bf16[128,256]{1,0:T(8,128)(2,1)S(1)}, bf16[128,256]{1,0:T(8,128)(2,1)S(1)}, u32[]{:S(2)}, u32[]{:S(2)}) %collective-permute-start.5) | collective-permute-done | bytes 65568 | tf_op jit(solution)/shard_map/ppermute | solution.py:295
  84.0 0.0 collective-permute-done.7
  84.0 0.0 collective-permute-done.6
  84.0 1.1 pad_maximum_fusion
  85.1 4.5 %all-to-all-start.2 = ((bf16[8,64,896]{2,1,0:T(8,128)(2,1)}), bf16[8,64,896]{2,1,0:T(8,128)(2,1)S(1)}, u32[]{:S(2)}, u32[]{:S(2)}) async-start(bf16[8,64,896]{2,1,0:T(8,128)(2,1)} %pad_maximum_fusion), calls=%async_computation.2 | async-start | bytes 1835008 | tf_op jit(solution)/shard_map/all_to_all | solution.py:255
  89.6 0.1 collective-permute-start.12
  89.7 0.4 collective-permute-start.11
  90.1 2.8 %collective-permute-start.10 = (bf16[128,256]{1,0:T(8,128)(2,1)S(1)}, bf16[128,256]{1,0:T(8,128)(2,1)S(1)}, u32[]{:S(2)}, u32[]{:S(2)}) collective-permute-start(bf16[128,256]{1,0:T(8,128)(2,1)S(1)} %add_convert_fusion.4), channel_id=1, source_target_pairs={{0,64},{64,128},{128,192},{192,0},{1,65},{65,129},{129,193},{193,1... | collective-permute-start | bytes 196616 | tf_op jit(solution)/shard_map/ppermute | solution.py:302
  92.9 2.9 %collective-permute-done.12 = bf16[128,256]{1,0:T(8,128)(2,1)S(1)} collective-permute-done((bf16[128,256]{1,0:T(8,128)(2,1)S(1)}, bf16[128,256]{1,0:T(8,128)(2,1)S(1)}, u32[]{:S(2)}, u32[]{:S(2)}) %collective-permute-start.12) | collective-permute-done | bytes 65568 | tf_op jit(solution)/shard_map/ppermute | solution.py:302
  95.9 0.0 collective-permute-done.11
  95.9 0.9 collective-permute-done.10
  96.7 0.7 add_convert_fusion.3
  97.4 6.2 %all-to-all-done.2.got = bf16[8,64,896]{2,1,0:T(8,128)(2,1)S(1)} async-done(((bf16[8,64,896]{2,1,0:T(8,128)(2,1)}), bf16[8,64,896]{2,1,0:T(8,128)(2,1)S(1)}, u32[]{:S(2)}, u32[]{:S(2)}) %all-to-all-start.2) | async-done | bytes 917536 | tf_op jit(solution)/shard_map/all_to_all | solution.py:255
  103.5 0.0 copy-start
  103.5 3.3 %all-to-all-start.3 = ((bf16[8,16,256]{2,1,0:T(8,128)(2,1)}), bf16[8,16,256]{2,1,0:T(8,128)(2,1)S(1)}, u32[]{:S(2)}, u32[]{:S(2)}) async-start(bf16[8,16,256]{2,1,0:T(8,128)(2,1)} %bitcast.4), calls=%async_computation.3 | async-start | bytes 131072 | tf_op jit(solution)/shard_map/all_to_all | solution.py:255
  106.9 0.0 copy-done
  106.9 2.1 %unpack_rows.1 = (bf16[2,64,2560]{2,1,0:T(8,128)(2,1)}, bf16[2,64,512]{2,1,0:T(8,128)(2,1)}, bf16[2,64,512]{2,1,0:T(8,128)(2,1)}) custom-call(bf16[8,64,896]{2,1,0:T(8,128)(2,1)} %copy-done), custom_call_target="tpu_custom_call" | custom-call | flops 1000 | bytes 2000000 | tf_op jit(solution)/shard_map/unpack_rows/pallas_call | solution.py:307
  109.1 4.1 %all-to-all-done.3.got = bf16[8,16,256]{2,1,0:T(8,128)(2,1)S(1)} async-done(((bf16[8,16,256]{2,1,0:T(8,128)(2,1)}), bf16[8,16,256]{2,1,0:T(8,128)(2,1)S(1)}, u32[]{:S(2)}, u32[]{:S(2)}) %all-to-all-start.3) | async-done | bytes 65568 | tf_op jit(solution)/shard_map/all_to_all | solution.py:255
  113.2 0.0 copy-start.1
  113.2 0.6 copy-done.1
  113.8 1.5 %unpack_prompt.1 = (bf16[16,512]{1,0:T(8,128)(2,1)}, bf16[16,512]{1,0:T(8,128)(2,1)}) custom-call(bf16[8,16,256]{2,1,0:T(8,128)(2,1)} %copy-done.1), custom_call_target="tpu_custom_call" | custom-call | flops 1000 | bytes 2000000 | tf_op jit(solution)/shard_map/unpack_prompt/pallas_call | solution.py:313
  (3 shorter events, 0.1 us)
Async XLA Ops:
  2.4 13.6 %all-to-all-start = ((bf16[8,80,256]{2,1,0:T(8,128)(2,1)}), bf16[8,80,256]{2,1,0:T(8,128)(2,1)S(1)}, u32[]{:S(2)}, u32[]{:S(2)}) async-start(bf16[8,80,256]{2,1,0:T(8,128)(2,1)} %pack_keys.1), calls=%async_computation | async-start | bytes 655360 | tf_op jit(solution)/shard_map/all_to_all | solution.py:255
  12.4 28.9 %copy-start.2 = (s32[2]{0:T(128)S(1)}, s32[2]{0:T(128)}, u32[]{:S(2)}) copy-start(s32[2]{0:T(128)} %param.15) | copy-start | bytes 28
  16.0 29.5 %all-to-all-start.1 = ((bf16[8,64,1408]{2,1,0:T(8,128)(2,1)}), bf16[8,64,1408]{2,1,0:T(8,128)(2,1)S(1)}, u32[]{:S(2)}, u32[]{:S(2)}) async-start(bf16[8,64,1408]{2,1,0:T(8,128)(2,1)} %pack_rows.1), calls=%async_computation.1 | async-start | bytes 2883584 | tf_op jit(solution)/shard_map/all_to_all | solution.py:255
  19.6 21.7 %collective-permute-start.1 = (bf16[8,80,256]{2,1,0:T(8,128)(2,1)S(1)}, bf16[8,80,256]{2,1,0:T(8,128)(2,1)S(1)}, u32[]{:S(2)}, u32[]{:S(2)}) collective-permute-start(bf16[8,80,256]{2,1,0:T(8,128)(2,1)S(1)} %all-to-all-done.refs_0_), channel_id=1, source_target_pairs={{0,4},{4,0},{1,5},{5,1},{2,6},{6,2},{3,7},{7,3},{8,12},{12,8},{9,1... | collective-permute-start | bytes 983048 | tf_op jit(solution)/shard_map/ppermute | solution.py:251
  23.0 19.6 %collective-permute-start = (bf16[8,80,256]{2,1,0:T(8,128)(2,1)S(1)}, bf16[8,80,256]{2,1,0:T(8,128)(2,1)S(1)}, u32[]{:S(2)}, u32[]{:S(2)}) collective-permute-start(bf16[8,80,256]{2,1,0:T(8,128)(2,1)S(1)} %all-to-all-done.refs_0_), channel_id=1, source_target_pairs={{0,1},{1,0},{2,3},{3,2},{4,5},{5,4},{6,7},{7,6},{8,9},{9,8},{10,11... | collective-permute-start | bytes 983048 | tf_op jit(solution)/shard_map/ppermute | solution.py:247
  41.3 1.6 %collective-permute-start.2 = (bf16[8,80,256]{2,1,0:T(8,128)(2,1)S(1)}, bf16[8,80,256]{2,1,0:T(8,128)(2,1)S(1)}, u32[]{:S(2)}, u32[]{:S(2)}) collective-permute-start(bf16[8,80,256]{2,1,0:T(8,128)(2,1)S(1)} %collective-permute-done.1.refs_2_), channel_id=1, source_target_pairs={{0,1},{1,0},{2,3},{3,2},{4,5},{5,4},{6,7},{7,6},{8,9},{9,8},{10,11... | collective-permute-start | bytes 983048 | tf_op jit(solution)/shard_map/ppermute | solution.py:247
  49.4 1.4 %collective-permute-start.4 = (bf16[256,256]{1,0:T(8,128)(2,1)S(1)}, bf16[256,256]{1,0:T(8,128)(2,1)S(1)}, u32[]{:S(2)}, u32[]{:S(2)}) collective-permute-start(bf16[256,256]{1,0:T(8,128)(2,1)S(1)} %get-tuple-element.29), channel_id=1, source_target_pairs={{0,1},{1,0},{2,3},{3,2},{4,5},{5,4},{6,7},{7,6},{8,9},{9,8},{10,11... | collective-permute-start | bytes 393224 | tf_op jit(solution)/shard_map/ppermute | solution.py:247
  49.5 1.7 %collective-permute-start.3 = (bf16[8,64,256]{2,1,0:T(8,128)(2,1)S(1)}, bf16[8,64,256]{2,1,0:T(8,128)(2,1)S(1)}, u32[]{:S(2)}, u32[]{:S(2)}) collective-permute-start(bf16[8,64,256]{2,1,0:T(8,128)(2,1)S(1)} %get-tuple-element.27), channel_id=1, source_target_pairs={{0,1},{1,0},{2,3},{3,2},{4,5},{5,4},{6,7},{7,6},{8,9},{9,8},{10,11... | collective-permute-start | bytes 786440 | tf_op jit(solution)/shard_map/ppermute | solution.py:247
  50.0 24.2 %collective-permute-start.8 = (bf16[8,64,256]{2,1,0:T(8,128)(2,1)S(1)}, bf16[8,64,256]{2,1,0:T(8,128)(2,1)S(1)}, u32[]{:S(2)}, u32[]{:S(2)}) collective-permute-start(bf16[8,64,256]{2,1,0:T(8,128)(2,1)S(1)} %get-tuple-element.32), channel_id=1, source_target_pairs={{0,1},{1,0},{2,3},{3,2},{4,5},{5,4},{6,7},{7,6},{8,9},{9,8},{10,11... | collective-permute-start | bytes 786440 | tf_op jit(solution)/shard_map/ppermute | solution.py:247
  51.3 22.9 %collective-permute-start.9 = (bf16[8,64,256]{2,1,0:T(8,128)(2,1)S(1)}, bf16[8,64,256]{2,1,0:T(8,128)(2,1)S(1)}, u32[]{:S(2)}, u32[]{:S(2)}) collective-permute-start(bf16[8,64,256]{2,1,0:T(8,128)(2,1)S(1)} %add_convert_fusion.1), channel_id=1, source_target_pairs={{0,4},{4,0},{1,5},{5,1},{2,6},{6,2},{3,7},{7,3},{8,12},{12,8},{9,1... | collective-permute-start | bytes 786440 | tf_op jit(solution)/shard_map/ppermute | solution.py:251
  51.4 32.6 %collective-permute-start.7 = (bf16[128,256]{1,0:T(8,128)(2,1)S(1)}, bf16[128,256]{1,0:T(8,128)(2,1)S(1)}, u32[]{:S(2)}, u32[]{:S(2)}) collective-permute-start(bf16[128,256]{1,0:T(8,128)(2,1)S(1)} %get-tuple-element.45), channel_id=1, source_target_pairs={{0,36},{4,32},{32,4},{36,0},{1,37},{5,33},{33,5},{37,1},{2,38},{6,... | collective-permute-start | bytes 196616 | tf_op jit(solution)/shard_map/ppermute | solution.py:295
  71.7 12.3 %collective-permute-start.6 = (bf16[128,256]{1,0:T(8,128)(2,1)S(1)}, bf16[128,256]{1,0:T(8,128)(2,1)S(1)}, u32[]{:S(2)}, u32[]{:S(2)}) collective-permute-start(bf16[128,256]{1,0:T(8,128)(2,1)S(1)} %get-tuple-element.45), channel_id=1, source_target_pairs={{0,4},{4,0},{32,36},{36,32},{1,5},{5,1},{33,37},{37,33},{2,6},{6,2... | collective-permute-start | bytes 196616 | tf_op jit(solution)/shard_map/ppermute | solution.py:295
  72.5 11.5 %collective-permute-start.5 = (bf16[128,256]{1,0:T(8,128)(2,1)S(1)}, bf16[128,256]{1,0:T(8,128)(2,1)S(1)}, u32[]{:S(2)}, u32[]{:S(2)}) collective-permute-start(bf16[128,256]{1,0:T(8,128)(2,1)S(1)} %get-tuple-element.46), channel_id=1, source_target_pairs={{0,32},{4,36},{32,0},{36,4},{1,33},{5,37},{33,1},{37,5},{2,34},{6,... | collective-permute-start | bytes 196616 | tf_op jit(solution)/shard_map/ppermute | solution.py:295
  85.1 18.5 %all-to-all-start.2 = ((bf16[8,64,896]{2,1,0:T(8,128)(2,1)}), bf16[8,64,896]{2,1,0:T(8,128)(2,1)S(1)}, u32[]{:S(2)}, u32[]{:S(2)}) async-start(bf16[8,64,896]{2,1,0:T(8,128)(2,1)} %pad_maximum_fusion), calls=%async_computation.2 | async-start | bytes 1835008 | tf_op jit(solution)/shard_map/all_to_all | solution.py:255
  89.6 6.3 %collective-permute-start.12 = (bf16[128,256]{1,0:T(8,128)(2,1)S(1)}, bf16[128,256]{1,0:T(8,128)(2,1)S(1)}, u32[]{:S(2)}, u32[]{:S(2)}) collective-permute-start(bf16[128,256]{1,0:T(8,128)(2,1)S(1)} %add_convert_fusion.4), channel_id=1, source_target_pairs={{0,192},{64,0},{128,64},{192,128},{1,193},{65,1},{129,65},{193,129... | collective-permute-start | bytes 196616 | tf_op jit(solution)/shard_map/ppermute | solution.py:302
  89.7 6.2 %collective-permute-start.11 = (bf16[128,256]{1,0:T(8,128)(2,1)S(1)}, bf16[128,256]{1,0:T(8,128)(2,1)S(1)}, u32[]{:S(2)}, u32[]{:S(2)}) collective-permute-start(bf16[128,256]{1,0:T(8,128)(2,1)S(1)} %add_convert_fusion.4), channel_id=1, source_target_pairs={{0,128},{64,192},{128,0},{192,64},{1,129},{65,193},{129,1},{193,65... | collective-permute-start | bytes 196616 | tf_op jit(solution)/shard_map/ppermute | solution.py:302
  90.1 6.6 %collective-permute-start.10 = (bf16[128,256]{1,0:T(8,128)(2,1)S(1)}, bf16[128,256]{1,0:T(8,128)(2,1)S(1)}, u32[]{:S(2)}, u32[]{:S(2)}) collective-permute-start(bf16[128,256]{1,0:T(8,128)(2,1)S(1)} %add_convert_fusion.4), channel_id=1, source_target_pairs={{0,64},{64,128},{128,192},{192,0},{1,65},{65,129},{129,193},{193,1... | collective-permute-start | bytes 196616 | tf_op jit(solution)/shard_map/ppermute | solution.py:302
  103.5 3.4 %copy-start = (bf16[8,64,896]{2,1,0:T(8,128)(2,1)}, bf16[8,64,896]{2,1,0:T(8,128)(2,1)S(1)}, u32[]{:S(2)}) copy-start(bf16[8,64,896]{2,1,0:T(8,128)(2,1)S(1)} %all-to-all-done.2.got) | copy-start | bytes 2752516
  103.5 9.6 %all-to-all-start.3 = ((bf16[8,16,256]{2,1,0:T(8,128)(2,1)}), bf16[8,16,256]{2,1,0:T(8,128)(2,1)S(1)}, u32[]{:S(2)}, u32[]{:S(2)}) async-start(bf16[8,16,256]{2,1,0:T(8,128)(2,1)} %bitcast.4), calls=%async_computation.3 | async-start | bytes 131072 | tf_op jit(solution)/shard_map/all_to_all | solution.py:255
  113.2 0.6 copy-start.1
where the time goes:
time: 115 us
  waiting for transfers between devices  49.8 us (43%)
  starting transfers between devices  47.3 us (41%)
  Pallas kernels  12 us (10%)
  local copies, waits for them, and re-layouts  2.8 us (2%)
  other arithmetic  2.68 us (2%)
    ppermute x3, starting transfers between devices, local(): lax.ppermute(part, ('hi', 'half'), [(i, i ^ mask) for i in range(4)])  22.8 us
    ppermute x2, waiting for transfers between devices, far(): return lax.ppermute(values, 'half', [(0, 1), (1, 0)])  18.3 us
    all_to_all x4, starting transfers between devices, exchange(): return lax.all_to_all(values, ('x', 'near'), 0, 0, tiled=True)  17.1 us
    all_to_all x4, waiting for transfers between devices, exchange(): return lax.all_to_all(values, ('x', 'near'), 0, 0, tiled=True)  16.6 us
    ppermute x3, waiting for transfers between devices, local(): lax.ppermute(part, ('hi', 'half'), [(i, i ^ mask) for i in range(4)])  9.67 us
    pallas_call x1, Pallas kernels, attend(): call(functools.partial(attend_kernel, 512), [shape((8, OWN, 2 * HD), BF)]...  3.88 us
    ppermute x3, waiting for transfers between devices, local(): lax.ppermute(prompt_sum, 'y', [(i, (i + by) % 4) for i in range(4)])  3.79 us
    ppermute x2, starting transfers between devices, far(): return lax.ppermute(values, 'half', [(0, 1), (1, 0)])  3.45 us
  transfers between devices with their start and end apart: 17, of which 11 were waited for; matrix products, arithmetic and copies ran while one was open for 3% of the time, Pallas kernels for 4%

commit v1 on v0

--- a/solution.py
+++ b/solution.py
@@ -233,14 +233,6 @@
             out_q[member, :, head * WIDE : (head + 1) * WIDE] = part[:, 0:WIDE]
             out_k[member, :, cols] = part[:, WIDE : WIDE + HD]
             out_v[member, :, cols] = part[:, WIDE + HD :]
-
-
-def unpack_prompt_kernel(got, out_k, out_v):
-    for head in range(4):
-        cols = slice(head * HD, (head + 1) * HD)
-        total = got[2 * head].astype(F32) + got[2 * head + 1].astype(F32)
-        out_k[:, cols] = total[:, 0:HD].astype(BF)
-        out_v[:, cols] = total[:, HD:].astype(BF)
 
 
 def swap(values):
@@ -310,9 +302,11 @@
         1,
         name="unpack_rows",
     )(back)
-    grad_prompt_keys, grad_prompt_values = call(
-        unpack_prompt_kernel, [shape((OWN_PROMPT, 4 * HD), BF)] * 2, 1, name="unpack_prompt"
-    )(prompt_back)
+    total = prompt_back.reshape(4, 2, OWN_PROMPT, 2 * HD).astype(F32)
+    total = (total[:, 0] + total[:, 1]).astype(BF)
+    total = jnp.concatenate([total[head] for head in range(4)], 1).reshape(OWN_PROMPT, 4, 2, HD)
+    grad_prompt_keys = total[:, :, 0].reshape(OWN_PROMPT, 4 * HD)
+    grad_prompt_values = total[:, :, 1].reshape(OWN_PROMPT, 4 * HD)
     return (grad_queries, grad_resp_keys, grad_resp_values, grad_prompt_keys, grad_prompt_values)
 
 

time: 115 us -> 112 us (0.974)
  the two profiles are of different devices: /device:TPU:24 before, /device:TPU:64 now
where the time goes in v1:
time: 112 us; the launch traced here: 110 us
  waiting for transfers between devices  45.9 us (41%)
  starting transfers between devices  43.8 us (39%)
  Pallas kernels  13.9 us (12%)
  local copies, waits for them, and re-layouts  2.98 us (3%)
  other arithmetic  2.72 us (2%)
    ppermute x2, waiting for transfers between devices, far(): return lax.ppermute(values, 'half', [(0, 1), (1, 0)])  30.8 us
    all_to_all x4, starting transfers between devices, exchange(): return lax.all_to_all(values, ('x', 'near'), 0, 0, tiled=True)  21.5 us
    ppermute x3, starting transfers between devices, local(): lax.ppermute(prompt_sum, 'y', [(i, (i + by) % 4) for i in range(4)])  11.8 us
    all_to_all x4, waiting for transfers between devices, exchange(): return lax.all_to_all(values, ('x', 'near'), 0, 0, tiled=True)  7.86 us
    pallas_call x1, Pallas kernels, attend(): call(functools.partial(attend_kernel, 512), [shape((8, OWN, 2 * HD), BF)]...  7.28 us
    ppermute x3, starting transfers between devices, local(): lax.ppermute(part, ('hi', 'half'), [(i, i ^ mask) for i in range(4)])  7.22 us
    ppermute x3, waiting for transfers between devices, local(): lax.ppermute(prompt_sum, 'y', [(i, (i + by) % 4) for i in range(4)])  5.22 us
    pallas_call x1, Pallas kernels, local(): call(pack_rows_kernel, shape((8, OWN, PACKED), BF), 3, name='pack_rows')  2.73 us
  transfers between devices with their start and end apart: 17, of which 11 were waited for; matrix products, arithmetic and copies ran while one was open for 3% of the time, Pallas kernels for 4%

profile of v1, /device:TPU:64, one launch (start us, length us, event | category | flops | bytes accessed | tf_op | source)
XLA Modules:
  0.0 110.1 jit_solution(16551646610582700117)
XLA Ops:
  0.6 1.8 %pack_keys.1 = bf16[8,80,256]{2,1,0:T(8,128)(2,1)} custom-call(bf16[2,64,512]{2,1,0:T(8,128)(2,1)} %k_ref.1, bf16[2,64,512]{2,1,0:T(8,128)(2,1)} %v_ref.1, bf16[16,512]{1,0:T(8,128)(2,1)} %pk_ref.1, bf16[16,512]{1,0:T(8,128)(2,1)} %pv_ref.1), custom_call_target="tpu_custom_call" | custom-call | flops 1000 | bytes 2000000 | tf_op jit(solution)/shard_map/pack_keys/pallas_call | solution.py:268
  2.4 5.7 %all-to-all-start = ((bf16[8,80,256]{2,1,0:T(8,128)(2,1)}), bf16[8,80,256]{2,1,0:T(8,128)(2,1)S(1)}, u32[]{:S(2)}, u32[]{:S(2)}) async-start(bf16[8,80,256]{2,1,0:T(8,128)(2,1)} %pack_keys.1), calls=%async_computation | async-start | bytes 655360 | tf_op jit(solution)/shard_map/all_to_all | solution.py:247
  8.0 1.6 %copy.14 = f32[2,64,4,5]{3,1,2,0:T(8,128)} copy(f32[2,64,4,5]{1,0,3,2:T(2,128)} %bitcast.29) | data formatting | bytes 20480 | tf_op jit(solution)/shard_map/reshape | solution.py:272
  9.6 2.7 %pack_rows.1 = bf16[8,64,1408]{2,1,0:T(8,128)(2,1)} custom-call(bf16[2,64,2560]{2,1,0:T(8,128)(2,1)} %q_ref.1, bf16[2,64,2560]{2,1,0:T(8,128)(2,1)} %c_ref.1, f32[2,4,64,5]{3,2,1,0:T(8,128)} %bitcast.25), custom_call_target="tpu_custom_call" | custom-call | flops 1000 | bytes 2000000 | tf_op jit(solution)/shard_map/pack_rows/pallas_call | solution.py:273
  12.4 0.0 copy-start.1
  12.4 3.7 %all-to-all-done.refs_0_ = bf16[8,80,256]{2,1,0:T(8,128)(2,1)S(1)} async-done(((bf16[8,80,256]{2,1,0:T(8,128)(2,1)}), bf16[8,80,256]{2,1,0:T(8,128)(2,1)S(1)}, u32[]{:S(2)}, u32[]{:S(2)}) %all-to-all-start) | async-done | bytes 327712 | tf_op jit(solution)/shard_map/all_to_all | solution.py:247
  16.0 3.6 %all-to-all-start.1 = ((bf16[8,64,1408]{2,1,0:T(8,128)(2,1)}), bf16[8,64,1408]{2,1,0:T(8,128)(2,1)S(1)}, u32[]{:S(2)}, u32[]{:S(2)}) async-start(bf16[8,64,1408]{2,1,0:T(8,128)(2,1)} %pack_rows.1), calls=%async_computation.1 | async-start | bytes 2883584 | tf_op jit(solution)/shard_map/all_to_all | solution.py:247
  19.6 0.1 collective-permute-start.1
  19.7 0.1 collective-permute-start
  19.8 21.6 %collective-permute-done.1.refs_2_ = bf16[8,80,256]{2,1,0:T(8,128)(2,1)S(1)} collective-permute-done((bf16[8,80,256]{2,1,0:T(8,128)(2,1)S(1)}, bf16[8,80,256]{2,1,0:T(8,128)(2,1)S(1)}, u32[]{:S(2)}, u32[]{:S(2)}) %collective-permute-start.1) | collective-permute-done | bytes 327712 | tf_op jit(solution)/shard_map/ppermute | solution.py:243
  41.4 0.0 collective-permute-start.2
  41.4 0.0 copy-done.1
  41.4 0.6 dynamic_slice.4
  42.0 0.7 pad_add_fusion.where
  42.7 0.0 collective-permute-done.refs_1_
  42.7 0.3 collective-permute-done.2.refs_3_
  43.0 0.0 all-to-all-done.1.refs_4_
  43.0 7.3 %attend.1 = (bf16[8,64,256]{2,1,0:T(8,128)(2,1)S(1)}, bf16[8,64,256]{2,1,0:T(8,128)(2,1)S(1)}, bf16[8,64,256]{2,1,0:T(8,128)(2,1)S(1)}, bf16[8,64,256]{2,1,0:T(8...) custom-call(s32[3]{0:T(128)S(1)} %pad_add_fusion.where, ...), custom_call_target="tpu_custom_call" | custom-call | flops 6000000000 | bytes 2000000 | tf_op jit(solution)/shard_map/attend/pallas_call | solution.py:203
  50.3 0.3 collective-permute-start.4
  50.6 0.3 collective-permute-start.3
  50.9 0.2 collective-permute-start.8
  51.1 0.6 collective-permute-done.4
  51.8 0.4 collective-permute-done.3
  52.1 0.1 add_convert_fusion.1
  52.2 2.3 %collective-permute-start.9 = (bf16[8,64,256]{2,1,0:T(8,128)(2,1)S(1)}, bf16[8,64,256]{2,1,0:T(8,128)(2,1)S(1)}, u32[]{:S(2)}, u32[]{:S(2)}) collective-permute-start(bf16[8,64,256]{2,1,0:T(8,128)(2,1)S(1)} %add_convert_fusion.1), channel_id=1, source_target_pairs={{0,4},{4,0},{1,5},{5,1},{2,6},{6,2},{3,7},{7,3},{8,12},{12,8},{9,1... | collective-permute-start | bytes 786440 | tf_op jit(solution)/shard_map/ppermute | solution.py:243
  54.5 4.8 %collective-permute-start.7 = (bf16[128,256]{1,0:T(8,128)(2,1)S(1)}, bf16[128,256]{1,0:T(8,128)(2,1)S(1)}, u32[]{:S(2)}, u32[]{:S(2)}) collective-permute-start(bf16[128,256]{1,0:T(8,128)(2,1)S(1)} %get-tuple-element.41), channel_id=1, source_target_pairs={{0,36},{4,32},{32,4},{36,0},{1,37},{5,33},{33,5},{37,1},{2,38},{6,... | collective-permute-start | bytes 196616 | tf_op jit(solution)/shard_map/ppermute | solution.py:287
  59.2 2.2 %collective-permute-start.6 = (bf16[128,256]{1,0:T(8,128)(2,1)S(1)}, bf16[128,256]{1,0:T(8,128)(2,1)S(1)}, u32[]{:S(2)}, u32[]{:S(2)}) collective-permute-start(bf16[128,256]{1,0:T(8,128)(2,1)S(1)} %get-tuple-element.41), channel_id=1, source_target_pairs={{0,4},{4,0},{32,36},{36,32},{1,5},{5,1},{33,37},{37,33},{2,6},{6,2... | collective-permute-start | bytes 196616 | tf_op jit(solution)/shard_map/ppermute | solution.py:287
  61.4 0.3 collective-permute-start.5
  61.7 0.0 collective-permute-done.8
  61.7 9.2 %collective-permute-done.9 = bf16[8,64,256]{2,1,0:T(8,128)(2,1)S(1)} collective-permute-done((bf16[8,64,256]{2,1,0:T(8,128)(2,1)S(1)}, bf16[8,64,256]{2,1,0:T(8,128)(2,1)S(1)}, u32[]{:S(2)}, u32[]{:S(2)}) %collective-permute-start.9) | collective-permute-done | bytes 262176 | tf_op jit(solution)/shard_map/ppermute | solution.py:243
  70.9 0.1 add_convert_fusion
  71.1 0.0 collective-permute-done.5
  71.1 0.0 collective-permute-done.7
  71.1 0.7 collective-permute-done.6
  71.8 1.1 pad_maximum_fusion
  72.8 6.6 %all-to-all-start.2 = ((bf16[8,64,896]{2,1,0:T(8,128)(2,1)}), bf16[8,64,896]{2,1,0:T(8,128)(2,1)S(1)}, u32[]{:S(2)}, u32[]{:S(2)}) async-start(bf16[8,64,896]{2,1,0:T(8,128)(2,1)} %pad_maximum_fusion), calls=%async_computation.2 | async-start | bytes 1835008 | tf_op jit(solution)/shard_map/all_to_all | solution.py:247
  79.5 10.9 %collective-permute-start.12 = (bf16[128,256]{1,0:T(8,128)(2,1)S(1)}, bf16[128,256]{1,0:T(8,128)(2,1)S(1)}, u32[]{:S(2)}, u32[]{:S(2)}) collective-permute-start(bf16[128,256]{1,0:T(8,128)(2,1)S(1)} %add_convert_fusion.4), channel_id=1, source_target_pairs={{0,192},{64,0},{128,64},{192,128},{1,193},{65,1},{129,65},{193,129... | collective-permute-start | bytes 196616 | tf_op jit(solution)/shard_map/ppermute | solution.py:294
  90.3 0.0 collective-permute-start.11
  90.3 1.0 collective-permute-start.10
  91.3 1.6 %collective-permute-done.12 = bf16[128,256]{1,0:T(8,128)(2,1)S(1)} collective-permute-done((bf16[128,256]{1,0:T(8,128)(2,1)S(1)}, bf16[128,256]{1,0:T(8,128)(2,1)S(1)}, u32[]{:S(2)}, u32[]{:S(2)}) %collective-permute-start.12) | collective-permute-done | bytes 65568 | tf_op jit(solution)/shard_map/ppermute | solution.py:294
  92.9 3.4 %collective-permute-done.11 = bf16[128,256]{1,0:T(8,128)(2,1)S(1)} collective-permute-done((bf16[128,256]{1,0:T(8,128)(2,1)S(1)}, bf16[128,256]{1,0:T(8,128)(2,1)S(1)}, u32[]{:S(2)}, u32[]{:S(2)}) %collective-permute-start.11) | collective-permute-done | bytes 65568 | tf_op jit(solution)/shard_map/ppermute | solution.py:294
  96.2 0.3 collective-permute-done.10
  96.5 0.7 add_convert_fusion.3
  97.2 0.0 all-to-all-done.2.got
  97.2 0.0 copy-start
  97.2 5.7 %all-to-all-start.3 = ((bf16[8,16,256]{2,1,0:T(8,128)(2,1)}), bf16[8,16,256]{2,1,0:T(8,128)(2,1)S(1)}, u32[]{:S(2)}, u32[]{:S(2)}) async-start(bf16[8,16,256]{2,1,0:T(8,128)(2,1)} %bitcast.4), calls=%async_computation.3 | async-start | bytes 131072 | tf_op jit(solution)/shard_map/all_to_all | solution.py:247
  102.9 0.0 copy-done
  102.9 2.1 %unpack_rows.1 = (bf16[2,64,2560]{2,1,0:T(8,128)(2,1)}, bf16[2,64,512]{2,1,0:T(8,128)(2,1)}, bf16[2,64,512]{2,1,0:T(8,128)(2,1)}) custom-call(bf16[8,64,896]{2,1,0:T(8,128)(2,1)} %copy-done), custom_call_target="tpu_custom_call" | custom-call | flops 1000 | bytes 2000000 | tf_op jit(solution)/shard_map/unpack_rows/pallas_call | solution.py:299
  105.0 4.2 %all-to-all-done.3 = bf16[8,16,256]{2,1,0:T(8,128)(2,1)S(1)} async-done(((bf16[8,16,256]{2,1,0:T(8,128)(2,1)}), bf16[8,16,256]{2,1,0:T(8,128)(2,1)S(1)}, u32[]{:S(2)}, u32[]{:S(2)}) %all-to-all-start.3) | async-done | bytes 65568 | tf_op jit(solution)/shard_map/all_to_all | solution.py:247
  109.4 0.1 fusion.2
  109.5 0.6 copy_bitcast_fusion
  (16 shorter events, 0.2 us)
Async XLA Ops:
  2.4 13.6 %all-to-all-start = ((bf16[8,80,256]{2,1,0:T(8,128)(2,1)}), bf16[8,80,256]{2,1,0:T(8,128)(2,1)S(1)}, u32[]{:S(2)}, u32[]{:S(2)}) async-start(bf16[8,80,256]{2,1,0:T(8,128)(2,1)} %pack_keys.1), calls=%async_computation | async-start | bytes 655360 | tf_op jit(solution)/shard_map/all_to_all | solution.py:247
  12.4 29.0 %copy-start.1 = (s32[2]{0:T(128)S(1)}, s32[2]{0:T(128)}, u32[]{:S(2)}) copy-start(s32[2]{0:T(128)} %param.15) | copy-start | bytes 28
  16.0 27.0 %all-to-all-start.1 = ((bf16[8,64,1408]{2,1,0:T(8,128)(2,1)}), bf16[8,64,1408]{2,1,0:T(8,128)(2,1)S(1)}, u32[]{:S(2)}, u32[]{:S(2)}) async-start(bf16[8,64,1408]{2,1,0:T(8,128)(2,1)} %pack_rows.1), calls=%async_computation.1 | async-start | bytes 2883584 | tf_op jit(solution)/shard_map/all_to_all | solution.py:247
  19.6 21.8 %collective-permute-start.1 = (bf16[8,80,256]{2,1,0:T(8,128)(2,1)S(1)}, bf16[8,80,256]{2,1,0:T(8,128)(2,1)S(1)}, u32[]{:S(2)}, u32[]{:S(2)}) collective-permute-start(bf16[8,80,256]{2,1,0:T(8,128)(2,1)S(1)} %all-to-all-done.refs_0_), channel_id=1, source_target_pairs={{0,4},{4,0},{1,5},{5,1},{2,6},{6,2},{3,7},{7,3},{8,12},{12,8},{9,1... | collective-permute-start | bytes 983048 | tf_op jit(solution)/shard_map/ppermute | solution.py:243
  19.7 23.0 %collective-permute-start = (bf16[8,80,256]{2,1,0:T(8,128)(2,1)S(1)}, bf16[8,80,256]{2,1,0:T(8,128)(2,1)S(1)}, u32[]{:S(2)}, u32[]{:S(2)}) collective-permute-start(bf16[8,80,256]{2,1,0:T(8,128)(2,1)S(1)} %all-to-all-done.refs_0_), channel_id=1, source_target_pairs={{0,1},{1,0},{2,3},{3,2},{4,5},{5,4},{6,7},{7,6},{8,9},{9,8},{10,11... | collective-permute-start | bytes 983048 | tf_op jit(solution)/shard_map/ppermute | solution.py:239
  41.4 1.6 %collective-permute-start.2 = (bf16[8,80,256]{2,1,0:T(8,128)(2,1)S(1)}, bf16[8,80,256]{2,1,0:T(8,128)(2,1)S(1)}, u32[]{:S(2)}, u32[]{:S(2)}) collective-permute-start(bf16[8,80,256]{2,1,0:T(8,128)(2,1)S(1)} %collective-permute-done.1.refs_2_), channel_id=1, source_target_pairs={{0,1},{1,0},{2,3},{3,2},{4,5},{5,4},{6,7},{7,6},{8,9},{9,8},{10,11... | collective-permute-start | bytes 983048 | tf_op jit(solution)/shard_map/ppermute | solution.py:239
  50.3 1.4 %collective-permute-start.4 = (bf16[256,256]{1,0:T(8,128)(2,1)S(1)}, bf16[256,256]{1,0:T(8,128)(2,1)S(1)}, u32[]{:S(2)}, u32[]{:S(2)}) collective-permute-start(bf16[256,256]{1,0:T(8,128)(2,1)S(1)} %get-tuple-element.27), channel_id=1, source_target_pairs={{0,1},{1,0},{2,3},{3,2},{4,5},{5,4},{6,7},{7,6},{8,9},{9,8},{10,11... | collective-permute-start | bytes 393224 | tf_op jit(solution)/shard_map/ppermute | solution.py:239
  50.6 1.5 %collective-permute-start.3 = (bf16[8,64,256]{2,1,0:T(8,128)(2,1)S(1)}, bf16[8,64,256]{2,1,0:T(8,128)(2,1)S(1)}, u32[]{:S(2)}, u32[]{:S(2)}) collective-permute-start(bf16[8,64,256]{2,1,0:T(8,128)(2,1)S(1)} %get-tuple-element.25), channel_id=1, source_target_pairs={{0,1},{1,0},{2,3},{3,2},{4,5},{5,4},{6,7},{7,6},{8,9},{9,8},{10,11... | collective-permute-start | bytes 786440 | tf_op jit(solution)/shard_map/ppermute | solution.py:239
  50.9 10.8 %collective-permute-start.8 = (bf16[8,64,256]{2,1,0:T(8,128)(2,1)S(1)}, bf16[8,64,256]{2,1,0:T(8,128)(2,1)S(1)}, u32[]{:S(2)}, u32[]{:S(2)}) collective-permute-start(bf16[8,64,256]{2,1,0:T(8,128)(2,1)S(1)} %get-tuple-element.30), channel_id=1, source_target_pairs={{0,1},{1,0},{2,3},{3,2},{4,5},{5,4},{6,7},{7,6},{8,9},{9,8},{10,11... | collective-permute-start | bytes 786440 | tf_op jit(solution)/shard_map/ppermute | solution.py:239
  52.2 18.7 %collective-permute-start.9 = (bf16[8,64,256]{2,1,0:T(8,128)(2,1)S(1)}, bf16[8,64,256]{2,1,0:T(8,128)(2,1)S(1)}, u32[]{:S(2)}, u32[]{:S(2)}) collective-permute-start(bf16[8,64,256]{2,1,0:T(8,128)(2,1)S(1)} %add_convert_fusion.1), channel_id=1, source_target_pairs={{0,4},{4,0},{1,5},{5,1},{2,6},{6,2},{3,7},{7,3},{8,12},{12,8},{9,1... | collective-permute-start | bytes 786440 | tf_op jit(solution)/shard_map/ppermute | solution.py:243
  54.5 16.6 %collective-permute-start.7 = (bf16[128,256]{1,0:T(8,128)(2,1)S(1)}, bf16[128,256]{1,0:T(8,128)(2,1)S(1)}, u32[]{:S(2)}, u32[]{:S(2)}) collective-permute-start(bf16[128,256]{1,0:T(8,128)(2,1)S(1)} %get-tuple-element.41), channel_id=1, source_target_pairs={{0,36},{4,32},{32,4},{36,0},{1,37},{5,33},{33,5},{37,1},{2,38},{6,... | collective-permute-start | bytes 196616 | tf_op jit(solution)/shard_map/ppermute | solution.py:287
  59.2 12.5 %collective-permute-start.6 = (bf16[128,256]{1,0:T(8,128)(2,1)S(1)}, bf16[128,256]{1,0:T(8,128)(2,1)S(1)}, u32[]{:S(2)}, u32[]{:S(2)}) collective-permute-start(bf16[128,256]{1,0:T(8,128)(2,1)S(1)} %get-tuple-element.41), channel_id=1, source_target_pairs={{0,4},{4,0},{32,36},{36,32},{1,5},{5,1},{33,37},{37,33},{2,6},{6,2... | collective-permute-start | bytes 196616 | tf_op jit(solution)/shard_map/ppermute | solution.py:287
  61.4 9.6 %collective-permute-start.5 = (bf16[128,256]{1,0:T(8,128)(2,1)S(1)}, bf16[128,256]{1,0:T(8,128)(2,1)S(1)}, u32[]{:S(2)}, u32[]{:S(2)}) collective-permute-start(bf16[128,256]{1,0:T(8,128)(2,1)S(1)} %get-tuple-element.42), channel_id=1, source_target_pairs={{0,32},{4,36},{32,0},{36,4},{1,33},{5,37},{33,1},{37,5},{2,34},{6,... | collective-permute-start | bytes 196616 | tf_op jit(solution)/shard_map/ppermute | solution.py:287
  72.8 24.3 %all-to-all-start.2 = ((bf16[8,64,896]{2,1,0:T(8,128)(2,1)}), bf16[8,64,896]{2,1,0:T(8,128)(2,1)S(1)}, u32[]{:S(2)}, u32[]{:S(2)}) async-start(bf16[8,64,896]{2,1,0:T(8,128)(2,1)} %pad_maximum_fusion), calls=%async_computation.2 | async-start | bytes 1835008 | tf_op jit(solution)/shard_map/all_to_all | solution.py:247
  79.5 13.4 %collective-permute-start.12 = (bf16[128,256]{1,0:T(8,128)(2,1)S(1)}, bf16[128,256]{1,0:T(8,128)(2,1)S(1)}, u32[]{:S(2)}, u32[]{:S(2)}) collective-permute-start(bf16[128,256]{1,0:T(8,128)(2,1)S(1)} %add_convert_fusion.4), channel_id=1, source_target_pairs={{0,192},{64,0},{128,64},{192,128},{1,193},{65,1},{129,65},{193,129... | collective-permute-start | bytes 196616 | tf_op jit(solution)/shard_map/ppermute | solution.py:294
  90.3 5.9 %collective-permute-start.11 = (bf16[128,256]{1,0:T(8,128)(2,1)S(1)}, bf16[128,256]{1,0:T(8,128)(2,1)S(1)}, u32[]{:S(2)}, u32[]{:S(2)}) collective-permute-start(bf16[128,256]{1,0:T(8,128)(2,1)S(1)} %add_convert_fusion.4), channel_id=1, source_target_pairs={{0,128},{64,192},{128,0},{192,64},{1,129},{65,193},{129,1},{193,65... | collective-permute-start | bytes 196616 | tf_op jit(solution)/shard_map/ppermute | solution.py:294
  90.3 6.2 %collective-permute-start.10 = (bf16[128,256]{1,0:T(8,128)(2,1)S(1)}, bf16[128,256]{1,0:T(8,128)(2,1)S(1)}, u32[]{:S(2)}, u32[]{:S(2)}) collective-permute-start(bf16[128,256]{1,0:T(8,128)(2,1)S(1)} %add_convert_fusion.4), channel_id=1, source_target_pairs={{0,64},{64,128},{128,192},{192,0},{1,65},{65,129},{129,193},{193,1... | collective-permute-start | bytes 196616 | tf_op jit(solution)/shard_map/ppermute | solution.py:294
  97.2 5.7 %copy-start = (bf16[8,64,896]{2,1,0:T(8,128)(2,1)}, bf16[8,64,896]{2,1,0:T(8,128)(2,1)S(1)}, u32[]{:S(2)}) copy-start(bf16[8,64,896]{2,1,0:T(8,128)(2,1)S(1)} %all-to-all-done.2.got) | copy-start | bytes 2752516
  97.2 12.1 %all-to-all-start.3 = ((bf16[8,16,256]{2,1,0:T(8,128)(2,1)}), bf16[8,16,256]{2,1,0:T(8,128)(2,1)S(1)}, u32[]{:S(2)}, u32[]{:S(2)}) async-start(bf16[8,16,256]{2,1,0:T(8,128)(2,1)} %bitcast.4), calls=%async_computation.3 | async-start | bytes 131072 | tf_op jit(solution)/shard_map/all_to_all | solution.py:247
